TPU v7x, 32 devices: a whole 2x2x4 slice. The times are simulated.
32 devices in a mesh: case: 2 (over y), wall: 4 (over z), azim: 4 (over x, core).
Axes of the slice: x: 2, y: 2, z: 4, core: 2. Of those that a mesh axis runs over, the one named last changes fastest.
Arguments:
- state: float32 [12, 2, 32, 512], P(None, 'case', 'wall', 'azim'), parts along dimension 1, may hold values from 0.5 to 1.5
- courant: float32 [2, 32, 512], P('case', 'wall', 'azim'), parts along dimension 0, may hold values from -0.6 to 0.6
- cross_sections: float32 [64], replicated, may hold values from 0.02 to 0.6
- band_fractions: float32 [64], replicated, may hold values from 0.02 to 0.2
- absorb_index: int32 [11, 16], replicated, may hold values from 0 to 63
- band_index: int32 [16], replicated, may hold values from 0 to 63
Outputs:
- new_state: float32 [12, 2, 32, 512], P(None, 'case', 'wall', 'azim'), parts along dimension 1
- wall_flux: float32 [2, 512], P('case', 'azim'), parts along dimension 0
There are 2 independent parts, one for each index of `case`. A program takes and returns all parts, laid end to end along the dimension named above; an argument that names none is the same for every part. Nothing has to cross between parts.
All inputs are finite; a program needn't handle non-finite values.
Results may differ from a plain program's by a relative error of at most 0.0003.
Values sent between devices are 32-bit elements; how exact they have to be, the bound alone decides.
A program may use at most 64 MiB of HBM per device.

v0:
```python
import jax
import jax.numpy as jnp
from jax import lax
from jax.sharding import PartitionSpec as P

KERNEL_WEIGHTS = (0.55, 0.45)
KERNEL_RATES = (1.15, 3.4)
FILTER_STRENGTH = 0.02
COUPLING = 0.1


def with_halo(block, sides, width):
    for axis, dim in sides:
        count = lax.axis_size(axis)
        forward = [(i, i + 1) for i in range(count - 1)]
        forward.append((count - 1, 0))
        backward = [(target, source) for source, target in forward]
        low = lax.ppermute(
            lax.slice_in_dim(block, block.shape[dim] - width, None, axis=dim), axis, forward
        )
        high = lax.ppermute(lax.slice_in_dim(block, 0, width, axis=dim), axis, backward)
        block = jnp.concatenate([low, block, high], axis=dim)
    return block


def band_tables(absorb_index, band_index, cross_sections, band_fractions):
    entries = cross_sections.shape[0]
    table_slots = lax.broadcasted_iota(jnp.int32, (1, 1, entries), 2)
    spectral_absorber_area = jnp.sum(
        jnp.where(absorb_index[:, :, None] == table_slots, cross_sections[None, None, :], 0.0),
        axis=2,
    )
    chosen_values = jnp.where(band_index[:, None] == table_slots[0], band_fractions[None, :], 0.0)
    return (spectral_absorber_area, jnp.sum(chosen_values, axis=1))


def viewing_line_irradiance(
    kinetic_heat_level,
    species_concentrations,
    spectral_absorber_area,
    spectral_fraction_weight,
    mesh_cell_width,
    viewing_line_dimension,
):
    absorption = jnp.einsum(
        "kb,kij->bij",
        spectral_absorber_area,
        species_concentrations,
        precision=lax.Precision.HIGHEST,
    )
    optical_thickness_step = absorption * mesh_cell_width
    optical_depth = (
        lax.cumsum(optical_thickness_step, viewing_line_dimension) - 0.5 * optical_thickness_step
    )
    radiated_energy_rate = (
        spectral_fraction_weight[:, None, None]
        * kinetic_heat_level[None] ** 4
        * optical_thickness_step
    )
    net_flux = 0.0
    wall_flux = 0.0
    for weight, decay_rate in zip(KERNEL_WEIGHTS, KERNEL_RATES):
        growth = jnp.exp(decay_rate * optical_depth)
        falloff = jnp.exp(-decay_rate * optical_depth)
        upward = falloff * lax.cumsum(radiated_energy_rate * growth, viewing_line_dimension)
        tail_sum = lax.cumsum(radiated_energy_rate * falloff, viewing_line_dimension, reverse=True)
        net_flux = net_flux + weight * jnp.sum(upward - growth * tail_sum, axis=0)
        wall_flux = wall_flux + weight * jnp.sum(
            lax.index_in_dim(tail_sum, 0, viewing_line_dimension, keepdims=False), axis=0
        )
    return (net_flux, wall_flux)


def edge_pad(net_flux, viewing_line_dimension):
    count = net_flux.shape[viewing_line_dimension]
    first_row = lax.slice_in_dim(net_flux, 0, 1, axis=viewing_line_dimension)
    last_row = lax.slice_in_dim(net_flux, count - 1, count, axis=viewing_line_dimension)
    return jnp.concatenate([first_row, net_flux, last_row], viewing_line_dimension)


def divergence(padded, viewing_line_dimension, mesh_cell_width):
    count = padded.shape[viewing_line_dimension] - 2
    before = lax.slice_in_dim(padded, 0, count, axis=viewing_line_dimension)
    after = lax.slice_in_dim(padded, 2, count + 2, axis=viewing_line_dimension)
    return (before - after) / (2.0 * mesh_cell_width)


def tendency(shifted, courant, heating):
    gradient = (
        45.0 * (shifted(1) - shifted(-1))
        - 9.0 * (shifted(2) - shifted(-2))
        + (shifted(3) - shifted(-3))
    ) / 60.0
    smoothing = (
        shifted(-3)
        + shifted(3)
        - 6.0 * (shifted(-2) + shifted(2))
        + 15.0 * (shifted(-1) + shifted(1))
        - 20.0 * shifted(0)
    )
    change_sum = FILTER_STRENGTH * smoothing - courant[None] * gradient
    return change_sum.at[0].add(COUPLING * heating)


def radiate(current, spectral_absorber_area, spectral_fraction_weight, mesh_cell_width):
    components, stations, row_count, col_count = current.shape
    line_data = jnp.transpose(current, (0, 2, 1, 3)).reshape(
        components, row_count, stations * col_count
    )
    gathered = lax.all_gather(line_data, "wall", axis=1, tiled=True)
    net_flux, wall_flux = viewing_line_irradiance(
        gathered[0],
        gathered[1:],
        spectral_absorber_area,
        spectral_fraction_weight,
        mesh_cell_width,
        1,
    )
    padded = edge_pad(net_flux, 0)
    row_start = lax.axis_index("wall") * row_count
    heating = divergence(
        lax.dynamic_slice_in_dim(padded, row_start, row_count + 2, 0), 0, mesh_cell_width
    )
    heating = jnp.transpose(heating.reshape(row_count, stations, col_count), (1, 0, 2))
    return (heating, wall_flux.reshape(stations, col_count))


def local(state, courant, cross_sections, band_fractions, absorb_index, band_index):
    spectral_absorber_area, spectral_fraction_weight = band_tables(
        absorb_index, band_index, cross_sections, band_fractions
    )
    mesh_cell_width = 1.0 / (state.shape[2] * lax.axis_size("wall"))
    col_count = state.shape[3]

    def segment_change(current):
        heating, wall_flux = radiate(
            current, spectral_absorber_area, spectral_fraction_weight, mesh_cell_width
        )
        padded = with_halo(current, (("azim", 3),), 3)

        def shifted(offset):
            return lax.slice_in_dim(padded, 3 + offset, 3 + offset + col_count, axis=3)

        return (tendency(shifted, courant, heating), wall_flux)

    first_change, first_flux = segment_change(state)
    middle = state + first_change
    second_change, second_flux = segment_change(middle)
    new_state = 0.5 * (state + middle + second_change)
    return (new_state, 0.5 * (first_flux + second_flux))


def solution(mesh):
    return jax.shard_map(
        local,
        mesh=mesh,
        in_specs=(P(None, "case", "wall", "azim"), P("case", "wall", "azim"), P(), P(), P(), P()),
        out_specs=(P(None, "case", "wall", "azim"), P("case", "azim")),
        check_vma=False,
    )
```

profile of v0, /device:TPU:0, one launch (start us, length us, event | category | flops | bytes accessed | tf_op | source)
XLA Modules:
  0.0 42.3 jit_solution(989441874617617582)
XLA Ops:
  0.6 1.0 %fusion.71 = (f32[12,1,8,3]{3,2,1,0:T(8,128)S(1)}, f32[12,1,8,3]{3,2,1,0:T(8,128)S(1)}) fusion(f32[12,1,8,128]{3,2,1,0:T(8,128)} %param.10), kind=kLoop, calls=%fused_computation.127 | loop fusion | bytes 4608 | tf_op jit(solution)/shard_map/slice | solution.py:21
  1.6 2.4 %collective-permute-start.1 = (f32[12,1,8,3]{3,2,1,0:T(8,128)S(1)}, f32[12,1,8,3]{3,2,1,0:T(8,128)S(1)}, u32[]{:S(2)}, u32[]{:S(2)}) collective-permute-start(f32[12,1,8,3]{3,2,1,0:T(8,128)S(1)} %get-tuple-element.34), channel_id=1, source_target_pairs={{1,0},{2,1},{3,2},{0,3},{5,4},{6,5},{7,6},{4,7},{9,8},{10,9},{11,1... | collective-permute-start | bytes 3464 | tf_op jit(solution)/shard_map/ppermute | solution.py:21
  4.0 0.1 copy.53
  4.1 14.1 %all-gather = f32[12,1,32,128]{3,1,0,2:T(1,128)S(1)} all-gather(f32[12,1,8,128]{3,1,0,2:T(1,128)S(1)} %copy.53), channel_id=2, replica_groups=mesh['case'=2,'wall'=4,'azim'=4] {'wall'}, dimensions={2}, use_global_device_ids=true | all-gather | bytes 245760 | tf_op jit(solution)/shard_map/all_gather | solution.py:110
  18.2 0.0 copy-start.1
  18.3 0.6 %copy-done.1 = s32[11,16]{1,0:T(8,128)S(1)} copy-done((s32[11,16]{1,0:T(8,128)S(1)}, s32[11,16]{1,0:T(8,128)}, u32[]{:S(2)}) %copy-start.1) | copy-done | bytes 728
  18.9 0.2 select_reduce_fusion
  19.1 0.4 fusion.5
  19.6 0.6 %copy-done.4 = f32[64]{0:T(128)S(1)} copy-done((f32[64]{0:T(128)S(1)}, f32[64]{0:T(128)}, u32[]{:S(2)}) %copy-start.4) | copy-done | bytes 280
  20.2 0.0 copy-done.5
  20.2 0.2 select_reduce_fusion.1
  20.4 0.2 fusion.16
  20.7 0.2 fusion.21
  20.9 0.2 fusion.74
  21.1 0.2 fusion.75
  21.4 0.7 %copy-done.2 = f32[1,8,128]{2,1,0:T(8,128)S(1)} copy-done((f32[1,8,128]{2,1,0:T(8,128)S(1)}, f32[1,8,128]{2,1,0:T(8,128)}, u32[]{:S(2)}) %copy-start.2) | copy-done | bytes 4120
  22.2 0.2 multiply_subtract_fusion.1
  22.4 0.1 copy.56
  22.5 0.1 fusion.70
  22.5 13.8 %all-gather.1 = f32[12,1,32,128]{3,1,0,2:T(1,128)S(1)} all-gather(f32[12,1,8,128]{3,1,0,2:T(1,128)S(1)} %copy.56), channel_id=3, replica_groups=mesh['case'=2,'wall'=4,'azim'=4] {'wall'}, dimensions={2}, use_global_device_ids=true | all-gather | bytes 245760 | tf_op jit(solution)/shard_map/all_gather | solution.py:110
  36.4 0.4 fusion.4
  36.8 0.2 fusion.6
  37.1 0.2 fusion.11
  37.3 0.2 fusion.76
  37.6 0.2 fusion.77
  37.8 0.1 collective-permute-start.3
  37.9 0.5 %collective-permute-start.2 = (f32[12,1,8,3]{3,2,1,0:T(8,128)S(1)}, f32[12,1,8,3]{3,2,1,0:T(8,128)S(1)}, u32[]{:S(2)}, u32[]{:S(2)}) collective-permute-start(f32[12,1,8,3]{3,2,1,0:T(8,128)S(1)} %get-tuple-element.33), channel_id=1, source_target_pairs={{0,1},{1,2},{2,3},{3,0},{4,5},{5,6},{6,7},{7,4},{8,9},{9,10},{10,1... | collective-permute-start | bytes 3464 | tf_op jit(solution)/shard_map/ppermute | solution.py:18
  38.4 0.5 %multiply_bitcast_fusion.1 = f32[1,128]{1,0:T(1,128)} fusion(f32[128]{0:T(128)S(1)} %get-tuple-element.40, f32[128]{0:T(128)S(1)} %get-tuple-element.41, f32[128]{0:T(128)S(1)} %get-tuple-element.42, f32[128]{0:T(128)S(1)} %get-tuple-element.43), kind=kLoop, calls=%fused_computation.115 | loop fusion | flops 1024 | bytes 2560 | tf_op jit(solution)/shard_map/mul | solution.py:150
  38.9 0.7 %collective-permute-done.3 = f32[12,1,8,3]{3,2,1,0:T(8,128)S(1)} collective-permute-done((f32[12,1,8,3]{3,2,1,0:T(8,128)S(1)}, f32[12,1,8,3]{3,2,1,0:T(8,128)S(1)}, u32[]{:S(2)}, u32[]{:S(2)}) %collective-permute-start.3) | collective-permute-done | bytes 1184 | tf_op jit(solution)/shard_map/ppermute | solution.py:21
  39.7 1.8 %collective-permute-done.2 = f32[12,1,8,3]{3,2,1,0:T(8,128)S(1)} collective-permute-done((f32[12,1,8,3]{3,2,1,0:T(8,128)S(1)}, f32[12,1,8,3]{3,2,1,0:T(8,128)S(1)}, u32[]{:S(2)}, u32[]{:S(2)}) %collective-permute-start.2) | collective-permute-done | bytes 1184 | tf_op jit(solution)/shard_map/ppermute | solution.py:18
  41.5 0.2 multiply_subtract_fusion
  41.7 0.6 %add_multiply_fusion = f32[12,1,8,128]{3,2,1,0:T(8,128)} fusion(f32[12,1,8,128]{3,2,1,0:T(8,128)S(1)} %fusion.55, f32[12,1,8,128]{3,2,1,0:T(8,128)S(1)} %copy-done, f32[12,1,8,128]{3,2,1,0:T(8,128)S(1)} %add.105), kind=kLoop, calls=%fused_computation.75 | loop fusion | flops 36864 | bytes 196608 | tf_op jit(solution)/shard_map/mul | solution.py:149
  (30 shorter events, 0.4 us)
Async XLA Ops:
  0.6 3.4 %copy-start = (f32[12,1,8,128]{3,2,1,0:T(8,128)S(1)}, f32[12,1,8,128]{3,2,1,0:T(8,128)}, u32[]{:S(2)}) copy-start(f32[12,1,8,128]{3,2,1,0:T(8,128)} %param.10) | copy-start | bytes 147460
  1.6 20.5 %collective-permute-start.1 = (f32[12,1,8,3]{3,2,1,0:T(8,128)S(1)}, f32[12,1,8,3]{3,2,1,0:T(8,128)S(1)}, u32[]{:S(2)}, u32[]{:S(2)}) collective-permute-start(f32[12,1,8,3]{3,2,1,0:T(8,128)S(1)} %get-tuple-element.34), channel_id=1, source_target_pairs={{1,0},{2,1},{3,2},{0,3},{5,4},{6,5},{7,6},{4,7},{9,8},{10,9},{11,1... | collective-permute-start | bytes 3464 | tf_op jit(solution)/shard_map/ppermute | solution.py:21
  4.0 18.2 %collective-permute-start = (f32[12,1,8,3]{3,2,1,0:T(8,128)S(1)}, f32[12,1,8,3]{3,2,1,0:T(8,128)S(1)}, u32[]{:S(2)}, u32[]{:S(2)}) collective-permute-start(f32[12,1,8,3]{3,2,1,0:T(8,128)S(1)} %get-tuple-element.35), channel_id=1, source_target_pairs={{0,1},{1,2},{2,3},{3,0},{4,5},{5,6},{6,7},{7,4},{8,9},{9,10},{10,1... | collective-permute-start | bytes 3464 | tf_op jit(solution)/shard_map/ppermute | solution.py:18
  18.2 0.7 %copy-start.1 = (s32[11,16]{1,0:T(8,128)S(1)}, s32[11,16]{1,0:T(8,128)}, u32[]{:S(2)}) copy-start(s32[11,16]{1,0:T(8,128)} %param.14) | copy-start | bytes 2116
  18.2 0.7 %copy-start.3 = (f32[64]{0:T(128)S(1)}, f32[64]{0:T(128)}, u32[]{:S(2)}) copy-start(f32[64]{0:T(128)} %param.12) | copy-start | bytes 772
  19.5 0.7 %copy-start.4 = (f32[64]{0:T(128)S(1)}, f32[64]{0:T(128)}, u32[]{:S(2)}) copy-start(f32[64]{0:T(128)} %param.13) | copy-start | bytes 772
  19.6 0.7 %copy-start.5 = (s32[16]{0:T(128)S(1)}, s32[16]{0:T(128)}, u32[]{:S(2)}) copy-start(s32[16]{0:T(128)} %param.15) | copy-start | bytes 196
  21.4 0.7 %copy-start.2 = (f32[1,8,128]{2,1,0:T(8,128)S(1)}, f32[1,8,128]{2,1,0:T(8,128)}, u32[]{:S(2)}) copy-start(f32[1,8,128]{2,1,0:T(8,128)} %param.11) | copy-start | bytes 12292
  37.8 1.8 %collective-permute-start.3 = (f32[12,1,8,3]{3,2,1,0:T(8,128)S(1)}, f32[12,1,8,3]{3,2,1,0:T(8,128)S(1)}, u32[]{:S(2)}, u32[]{:S(2)}) collective-permute-start(f32[12,1,8,3]{3,2,1,0:T(8,128)S(1)} %get-tuple-element.32), channel_id=1, source_target_pairs={{1,0},{2,1},{3,2},{0,3},{5,4},{6,5},{7,6},{4,7},{9,8},{10,9},{11,1... | collective-permute-start | bytes 3464 | tf_op jit(solution)/shard_map/ppermute | solution.py:21
  37.9 3.6 %collective-permute-start.2 = (f32[12,1,8,3]{3,2,1,0:T(8,128)S(1)}, f32[12,1,8,3]{3,2,1,0:T(8,128)S(1)}, u32[]{:S(2)}, u32[]{:S(2)}) collective-permute-start(f32[12,1,8,3]{3,2,1,0:T(8,128)S(1)} %get-tuple-element.33), channel_id=1, source_target_pairs={{0,1},{1,2},{2,3},{3,0},{4,5},{5,6},{6,7},{7,4},{8,9},{9,10},{10,1... | collective-permute-start | bytes 3464 | tf_op jit(solution)/shard_map/ppermute | solution.py:18
where the time goes:
time: 42.6 us; the launch traced here: 42.3 us
  blocking collectives  27.9 us (65%)
  other arithmetic  4.04 us (9%)
  local copies, waits for them, and re-layouts  3.18 us (7%)
  starting transfers between devices  2.94 us (7%)
  waiting for transfers between devices  2.52 us (6%)
  between operations  0.89 us (2%)
  matrix products  0.84 us (2%)
    all_gather x2, blocking collectives, radiate(): gathered = lax.all_gather(line_data, 'wall', axis=1, tiled=True)  27.9 us
    ppermute x2, starting transfers between devices, with_halo(): lax.ppermute(lax.slice_in_dim(block, 0, width, axis=dim), axis, backward)  2.44 us
    unnamed x14, local copies, waits for them, and re-layouts  2 us
    ppermute x2, waiting for transfers between devices, with_halo(): lax.ppermute(lax.slice_in_dim(block, block.shape[dim] - width, None, axis...  1.79 us
    slice x2, local copies, waits for them, and re-layouts, with_halo(): lax.slice_in_dim(block, 0, width, axis=dim)  1.05 us
    another operation x6, other arithmetic, viewing_line_irradiance(): lax.cumsum(optical_thickness_step, viewing_line_dimension)  1.01 us
    another operation x4, other arithmetic, viewing_line_irradiance(): lax.cumsum(radiated_energy_rate * falloff, viewing_line_dimension, revers...  0.98 us
  transfers between devices with their start and end apart: 4, of which 2 were waited for; matrix products, arithmetic and copies ran while one was open for 6% of the time, Pallas kernels for 0%

commit v1 on v0

--- a/solution.py
+++ b/solution.py
@@ -107,7 +107,15 @@
     line_data = jnp.transpose(current, (0, 2, 1, 3)).reshape(
         components, row_count, stations * col_count
     )
-    gathered = lax.all_gather(line_data, "wall", axis=1, tiled=True)
+    ways, here, lap = (lax.axis_size("wall"), lax.axis_index("wall"), line_data.shape[1])
+    line, have = (line_data, 1)
+    while have < ways:
+        line = jnp.concatenate(
+            [line, lax.ppermute(line, "wall", [(d, (d - have) % ways) for d in range(ways)])],
+            axis=1,
+        )
+        have = 2 * have
+    gathered = jnp.roll(line, here * lap, axis=1)
     net_flux, wall_flux = viewing_line_irradiance(
         gathered[0],
         gathered[1:],

time: 42.6 us -> 35 us (0.82)
  blocking collectives: 27.9 us -> 0 us
  waiting for transfers between devices: 2.52 us -> 15.8 us
  starting transfers between devices: 2.94 us -> 9.93 us
    all_gather x2 -> x0, blocking collectives: 27.9 us -> none  [radiate(): gathered = lax.all_gather(line_data, 'wall', axis=1, tiled=True)]
    ppermute x0 -> x4, waiting for transfers between devices: none -> 13.3 us  [radiate(): lax.ppermute(line, 'wall', [(d, (d - have) % ways) for d in range(ways)])]
    ppermute x0 -> x4, starting transfers between devices: none -> 8.5 us  [radiate(): lax.ppermute(line, 'wall', [(d, (d - have) % ways) for d in range(ways)])]
    ppermute x2, starting transfers between devices: 2.44 us -> 1.43 us  [with_halo(): lax.ppermute(lax.slice_in_dim(block, 0, width, axis=dim), axis, backward)]
    slice x2, local copies, waits for them, and re-layouts: 1.05 us -> 0.15 us  [with_halo(): lax.slice_in_dim(block, 0, width, axis=dim)]
    ppermute x2, waiting for transfers between devices: 0.73 us -> 0.01 us  [with_halo(): lax.ppermute(lax.slice_in_dim(block, 0, width, axis=dim), axis, backward)]
    ppermute x2, waiting for transfers between devices: 1.79 us -> 2.51 us  [with_halo(): lax.ppermute(lax.slice_in_dim(block, block.shape[dim] - width, None, axis...]
    unnamed x14, local copies, waits for them, and re-layouts: 2 us -> 2.69 us
  transfers between devices with their start and end apart: 4 -> 8, of which waited for: 2 -> 5; matrix products, arithmetic and copies ran while one was open for 6% -> 2% of each run, Pallas kernels for 0% -> 0%
where the time goes in v1:
time: 35 us; the launch traced here: 34.8 us
  waiting for transfers between devices  15.8 us (45%)
  starting transfers between devices  9.93 us (28%)
  other arithmetic  4.44 us (13%)
  local copies, waits for them, and re-layouts  2.87 us (8%)
  between operations  0.9 us (3%)
  matrix products  0.88 us (3%)
    ppermute x4, waiting for transfers between devices, radiate(): lax.ppermute(line, 'wall', [(d, (d - have) % ways) for d in range(ways)])  13.3 us
    ppermute x4, starting transfers between devices, radiate(): lax.ppermute(line, 'wall', [(d, (d - have) % ways) for d in range(ways)])  8.5 us
    unnamed x14, local copies, waits for them, and re-layouts  2.69 us
    ppermute x2, waiting for transfers between devices, with_halo(): lax.ppermute(lax.slice_in_dim(block, block.shape[dim] - width, None, axis...  2.51 us
    ppermute x2, starting transfers between devices, with_halo(): lax.ppermute(lax.slice_in_dim(block, 0, width, axis=dim), axis, backward)  1.43 us
    another operation x6, other arithmetic, viewing_line_irradiance(): lax.cumsum(optical_thickness_step, viewing_line_dimension)  1.01 us
    another operation x4, other arithmetic, viewing_line_irradiance(): lax.cumsum(radiated_energy_rate * falloff, viewing_line_dimension, revers...  0.98 us
    dot_general x2, matrix products, viewing_line_irradiance(): jnp.einsum('kb,kij->bij', spectral_absorber_area, species_concentrations,...  0.88 us
  transfers between devices with their start and end apart: 8, of which 5 were waited for; matrix products, arithmetic and copies ran while one was open for 2% of the time, Pallas kernels for 0%

profile of v1, /device:TPU:0, one launch (start us, length us, event | category | flops | bytes accessed | tf_op | source)
XLA Modules:
  0.0 34.8 jit_solution(11101532687154516964)
XLA Ops:
  0.6 0.9 %copy.47 = f32[12,1,8,128]{3,0,2,1:T(8,128)S(1)} copy(f32[12,1,8,128]{3,2,1,0:T(8,128)} %param.12) | data formatting | bytes 98304 | tf_op args[0]
  1.5 5.1 %collective-permute-start.2 = (f32[12,8,128]{2,0,1:T(8,128)S(1)}, f32[12,8,128]{2,0,1:T(8,128)S(1)}, u32[]{:S(2)}, u32[]{:S(2)}) collective-permute-start(f32[12,8,128]{2,0,1:T(8,128)S(1)} %bitcast.32), channel_id=1, source_target_pairs={{0,12},{4,0},{8,4},{12,8},{1,13},{5,1},{9,5},{13,9},{2,14},{6,2},{... | collective-permute-start | bytes 147464 | tf_op jit(solution)/shard_map/ppermute | solution.py:114
  6.7 0.7 %collective-permute-start.1 = (f32[12,1,8,3]{3,2,1,0:T(8,128)S(1)}, f32[12,1,8,3]{3,2,1,0:T(8,128)S(1)}, u32[]{:S(2)}, u32[]{:S(2)}) collective-permute-start(f32[12,1,8,3]{3,2,1,0:T(8,128)S(1)} %get-tuple-element.33), channel_id=1, source_target_pairs={{1,0},{2,1},{3,2},{0,3},{5,4},{6,5},{7,6},{4,7},{9,8},{10,9},{11,1... | collective-permute-start | bytes 3464 | tf_op jit(solution)/shard_map/ppermute | solution.py:21
  7.4 0.7 %copy-done.2 = f32[1,8,128]{2,1,0:T(8,128)S(1)} copy-done((f32[1,8,128]{2,1,0:T(8,128)S(1)}, f32[1,8,128]{2,1,0:T(8,128)}, u32[]{:S(2)}) %copy-start.2) | copy-done | bytes 4120
  8.1 0.6 %copy-done.4 = f32[64]{0:T(128)S(1)} copy-done((f32[64]{0:T(128)S(1)}, f32[64]{0:T(128)}, u32[]{:S(2)}) %copy-start.4) | copy-done | bytes 280
  8.7 0.2 select_reduce_fusion.1
  8.9 0.5 %copy-done.3 = f32[64]{0:T(128)S(1)} copy-done((f32[64]{0:T(128)S(1)}, f32[64]{0:T(128)}, u32[]{:S(2)}) %copy-start.3) | copy-done | bytes 280
  9.4 0.2 select_reduce_fusion
  9.6 0.3 collective-permute-start.3
  9.9 0.9 %collective-permute-done = f32[12,1,8,3]{3,2,1,0:T(8,128)S(1)} collective-permute-done((f32[12,1,8,3]{3,2,1,0:T(8,128)S(1)}, f32[12,1,8,3]{3,2,1,0:T(8,128)S(1)}, u32[]{:S(2)}, u32[]{:S(2)}) %collective-permute-start) | collective-permute-done | bytes 1184 | tf_op jit(solution)/shard_map/ppermute | solution.py:18
  10.9 0.2 multiply_subtract_fusion.1
  11.1 7.3 %collective-permute-done.3 = f32[12,16,128]{2,0,1:T(8,128)S(1)} collective-permute-done((f32[12,16,128]{2,0,1:T(8,128)S(1)}, f32[12,16,128]{2,0,1:T(8,128)S(1)}, u32[]{:S(2)}, u32[]{:S(2)}) %collective-permute-start.3) | collective-permute-done | bytes 98336 | tf_op jit(solution)/shard_map/ppermute | solution.py:114
  18.3 0.3 fusion.6
  18.7 0.4 %fusion.9 = f32[16,32,128]{2,0,1:T(8,128)S(1)} fusion(f32[12,32,128]{2,0,1:T(8,128)S(1)} %fusion.6, f32[11,16]{1,0:T(8,128)S(1)} %select_reduce_fusion), kind=kOutput, calls=%fused_computation.27 | convolution fusion | flops 8650752 | bytes 459456 | tf_op jit(solution)/shard_map/kb,kij->bij/dot_general | solution.py:45
  19.1 0.2 fusion.23
  19.4 0.2 fusion.28
  19.6 0.2 fusion.85
  19.9 0.2 fusion.86
  20.3 2.2 %collective-permute-start.6 = (f32[12,8,128]{2,1,0:T(8,128)S(1)}, f32[12,8,128]{2,1,0:T(8,128)S(1)}, u32[]{:S(2)}, u32[]{:S(2)}) collective-permute-start(f32[12,8,128]{2,1,0:T(8,128)S(1)} %bitcast.29), channel_id=1, source_target_pairs={{0,12},{4,0},{8,4},{12,8},{1,13},{5,1},{9,5},{13,9},{2,14},{6,2},{... | collective-permute-start | bytes 147464 | tf_op jit(solution)/shard_map/ppermute | solution.py:114
  22.5 0.8 %collective-permute-start.5 = (f32[12,1,8,3]{3,2,1,0:T(8,128)S(1)}, f32[12,1,8,3]{3,2,1,0:T(8,128)S(1)}, u32[]{:S(2)}, u32[]{:S(2)}) collective-permute-start(f32[12,1,8,3]{3,2,1,0:T(8,128)S(1)} %get-tuple-element.31), channel_id=1, source_target_pairs={{1,0},{2,1},{3,2},{0,3},{5,4},{6,5},{7,6},{4,7},{9,8},{10,9},{11,1... | collective-permute-start | bytes 3464 | tf_op jit(solution)/shard_map/ppermute | solution.py:21
  23.3 1.1 %collective-permute-done.6 = f32[12,8,128]{2,1,0:T(8,128)S(1)} collective-permute-done((f32[12,8,128]{2,1,0:T(8,128)S(1)}, f32[12,8,128]{2,1,0:T(8,128)S(1)}, u32[]{:S(2)}, u32[]{:S(2)}) %collective-permute-start.6) | collective-permute-done | bytes 49184 | tf_op jit(solution)/shard_map/ppermute | solution.py:114
  24.4 0.8 %collective-permute-start.7 = (f32[12,16,128]{2,1,0:T(8,128)S(1)}, f32[12,16,128]{2,1,0:T(8,128)S(1)}, u32[]{:S(2)}, u32[]{:S(2)}) collective-permute-start(f32[12,16,128]{2,1,0:T(8,128)S(1)} %pad_maximum_fusion.1), channel_id=1, source_target_pairs={{0,8},{4,12},{8,0},{12,4},{1,9},{5,13},{9,1},{13,5},{2,10},{6,14},... | collective-permute-start | bytes 294920 | tf_op jit(solution)/shard_map/ppermute | solution.py:114
  25.2 1.6 %collective-permute-done.4 = f32[12,1,8,3]{3,2,1,0:T(8,128)S(1)} collective-permute-done((f32[12,1,8,3]{3,2,1,0:T(8,128)S(1)}, f32[12,1,8,3]{3,2,1,0:T(8,128)S(1)}, u32[]{:S(2)}, u32[]{:S(2)}) %collective-permute-start.4) | collective-permute-done | bytes 1184 | tf_op jit(solution)/shard_map/ppermute | solution.py:18
  26.8 0.2 multiply_subtract_fusion
  27.0 4.9 %collective-permute-done.7 = f32[12,16,128]{2,1,0:T(8,128)S(1)} collective-permute-done((f32[12,16,128]{2,1,0:T(8,128)S(1)}, f32[12,16,128]{2,1,0:T(8,128)S(1)}, u32[]{:S(2)}, u32[]{:S(2)}) %collective-permute-start.7) | collective-permute-done | bytes 98336 | tf_op jit(solution)/shard_map/ppermute | solution.py:114
  32.1 0.5 %fusion.11 = f32[16,32,128]{2,0,1:T(8,128)S(1)} fusion(f32[11,32,128]{2,1,0:T(8,128)S(1)} %slice.233, f32[11,16]{1,0:T(8,128)S(1)} %select_reduce_fusion), kind=kOutput, calls=%fused_computation.29 | convolution fusion | flops 8650752 | bytes 443072 | tf_op jit(solution)/shard_map/kb,kij->bij/dot_general | solution.py:45
  32.6 0.2 fusion.13
  32.8 0.2 fusion.18
  33.1 0.2 fusion.87
  33.3 0.2 fusion.88
  33.7 0.6 %add_multiply_fusion = f32[12,1,8,128]{3,2,1,0:T(8,128)} fusion(f32[12,1,8,128]{3,2,1,0:T(8,128)S(1)} %constant_dynamic-update-slice_fusion.2, f32[12,1,8,128]{3,2,1,0:T(8,128)S(1)} %copy-done, f32[12,1,8,128]{3,2,1,0:T(8,128)S(1)} %add.113), kind=kLoop, calls=%fused_computation.100 | loop fusion | flops 36864 | bytes 196608 | tf_op jit(solution)/shard_map/mul | solution.py:157
  34.3 0.5 %multiply_bitcast_fusion.1 = f32[1,128]{1,0:T(1,128)} fusion(f32[128]{0:T(128)S(1)} %get-tuple-element.39, f32[128]{0:T(128)S(1)} %get-tuple-element.40, f32[128]{0:T(128)S(1)} %get-tuple-element.41, f32[128]{0:T(128)S(1)} %get-tuple-element.42), kind=kLoop, calls=%fused_computation.141 | loop fusion | flops 1024 | bytes 2560 | tf_op jit(solution)/shard_map/mul | solution.py:158
  (38 shorter events, 0.6 us)
Async XLA Ops:
  0.6 6.0 %copy-start = (f32[12,1,8,128]{3,2,1,0:T(8,128)S(1)}, f32[12,1,8,128]{3,2,1,0:T(8,128)}, u32[]{:S(2)}) copy-start(f32[12,1,8,128]{3,2,1,0:T(8,128)} %param.12) | copy-start | bytes 147460
  1.5 8.1 %collective-permute-start.2 = (f32[12,8,128]{2,0,1:T(8,128)S(1)}, f32[12,8,128]{2,0,1:T(8,128)S(1)}, u32[]{:S(2)}, u32[]{:S(2)}) collective-permute-start(f32[12,8,128]{2,0,1:T(8,128)S(1)} %bitcast.32), channel_id=1, source_target_pairs={{0,12},{4,0},{8,4},{12,8},{1,13},{5,1},{9,5},{13,9},{2,14},{6,2},{... | collective-permute-start | bytes 147464 | tf_op jit(solution)/shard_map/ppermute | solution.py:114
  6.7 2.9 %collective-permute-start.1 = (f32[12,1,8,3]{3,2,1,0:T(8,128)S(1)}, f32[12,1,8,3]{3,2,1,0:T(8,128)S(1)}, u32[]{:S(2)}, u32[]{:S(2)}) collective-permute-start(f32[12,1,8,3]{3,2,1,0:T(8,128)S(1)} %get-tuple-element.33), channel_id=1, source_target_pairs={{1,0},{2,1},{3,2},{0,3},{5,4},{6,5},{7,6},{4,7},{9,8},{10,9},{11,1... | collective-permute-start | bytes 3464 | tf_op jit(solution)/shard_map/ppermute | solution.py:21
  7.4 3.5 %collective-permute-start = (f32[12,1,8,3]{3,2,1,0:T(8,128)S(1)}, f32[12,1,8,3]{3,2,1,0:T(8,128)S(1)}, u32[]{:S(2)}, u32[]{:S(2)}) collective-permute-start(f32[12,1,8,3]{3,2,1,0:T(8,128)S(1)} %get-tuple-element.34), channel_id=1, source_target_pairs={{0,1},{1,2},{2,3},{3,0},{4,5},{5,6},{6,7},{7,4},{8,9},{9,10},{10,1... | collective-permute-start | bytes 3464 | tf_op jit(solution)/shard_map/ppermute | solution.py:18
  7.4 0.7 %copy-start.2 = (f32[1,8,128]{2,1,0:T(8,128)S(1)}, f32[1,8,128]{2,1,0:T(8,128)}, u32[]{:S(2)}) copy-start(f32[1,8,128]{2,1,0:T(8,128)} %param.13) | copy-start | bytes 12292
  7.4 1.5 %copy-start.1 = (s32[11,16]{1,0:T(8,128)S(1)}, s32[11,16]{1,0:T(8,128)}, u32[]{:S(2)}) copy-start(s32[11,16]{1,0:T(8,128)} %param.16) | copy-start | bytes 2116
  8.0 0.7 %copy-start.4 = (f32[64]{0:T(128)S(1)}, f32[64]{0:T(128)}, u32[]{:S(2)}) copy-start(f32[64]{0:T(128)} %param.15) | copy-start | bytes 772
  8.0 0.7 %copy-start.5 = (s32[16]{0:T(128)S(1)}, s32[16]{0:T(128)}, u32[]{:S(2)}) copy-start(s32[16]{0:T(128)} %param.17) | copy-start | bytes 196
  8.7 0.7 %copy-start.3 = (f32[64]{0:T(128)S(1)}, f32[64]{0:T(128)}, u32[]{:S(2)}) copy-start(f32[64]{0:T(128)} %param.14) | copy-start | bytes 772
  9.6 8.7 %collective-permute-start.3 = (f32[12,16,128]{2,0,1:T(8,128)S(1)}, f32[12,16,128]{2,0,1:T(8,128)S(1)}, u32[]{:S(2)}, u32[]{:S(2)}) collective-permute-start(f32[12,16,128]{2,0,1:T(8,128)S(1)} %pad_maximum_fusion), channel_id=1, source_target_pairs={{0,8},{4,12},{8,0},{12,4},{1,9},{5,13},{9,1},{13,5},{2,10},{6,14},... | collective-permute-start | bytes 294920 | tf_op jit(solution)/shard_map/ppermute | solution.py:114
  20.3 4.1 %collective-permute-start.6 = (f32[12,8,128]{2,1,0:T(8,128)S(1)}, f32[12,8,128]{2,1,0:T(8,128)S(1)}, u32[]{:S(2)}, u32[]{:S(2)}) collective-permute-start(f32[12,8,128]{2,1,0:T(8,128)S(1)} %bitcast.29), channel_id=1, source_target_pairs={{0,12},{4,0},{8,4},{12,8},{1,13},{5,1},{9,5},{13,9},{2,14},{6,2},{... | collective-permute-start | bytes 147464 | tf_op jit(solution)/shard_map/ppermute | solution.py:114
  22.5 2.7 %collective-permute-start.5 = (f32[12,1,8,3]{3,2,1,0:T(8,128)S(1)}, f32[12,1,8,3]{3,2,1,0:T(8,128)S(1)}, u32[]{:S(2)}, u32[]{:S(2)}) collective-permute-start(f32[12,1,8,3]{3,2,1,0:T(8,128)S(1)} %get-tuple-element.31), channel_id=1, source_target_pairs={{1,0},{2,1},{3,2},{0,3},{5,4},{6,5},{7,6},{4,7},{9,8},{10,9},{11,1... | collective-permute-start | bytes 3464 | tf_op jit(solution)/shard_map/ppermute | solution.py:21
  23.3 3.5 %collective-permute-start.4 = (f32[12,1,8,3]{3,2,1,0:T(8,128)S(1)}, f32[12,1,8,3]{3,2,1,0:T(8,128)S(1)}, u32[]{:S(2)}, u32[]{:S(2)}) collective-permute-start(f32[12,1,8,3]{3,2,1,0:T(8,128)S(1)} %get-tuple-element.32), channel_id=1, source_target_pairs={{0,1},{1,2},{2,3},{3,0},{4,5},{5,6},{6,7},{7,4},{8,9},{9,10},{10,1... | collective-permute-start | bytes 3464 | tf_op jit(solution)/shard_map/ppermute | solution.py:18
  24.4 7.6 %collective-permute-start.7 = (f32[12,16,128]{2,1,0:T(8,128)S(1)}, f32[12,16,128]{2,1,0:T(8,128)S(1)}, u32[]{:S(2)}, u32[]{:S(2)}) collective-permute-start(f32[12,16,128]{2,1,0:T(8,128)S(1)} %pad_maximum_fusion.1), channel_id=1, source_target_pairs={{0,8},{4,12},{8,0},{12,4},{1,9},{5,13},{9,1},{13,5},{2,10},{6,14},... | collective-permute-start | bytes 294920 | tf_op jit(solution)/shard_map/ppermute | solution.py:114
